TPU v7x, 32 devices: a whole 2x2x4 slice. The times are simulated.
32 devices in a mesh: wide: 8 (over y, x, core), narrow: 4 (over z).
Axes of the slice: x: 2, y: 2, z: 4, core: 2. Of those that a mesh axis runs over, the one named last changes fastest.
Arguments:
- tokens_in: bfloat16 [640, 24576], P('narrow', 'wide'), may hold values from -6 to 6
- ln1_gain: bfloat16 [640], P('narrow'), may hold values from 0.25 to 1.75
- ln1_shift: bfloat16 [640], P('narrow'), may hold values from -3 to 3
- w_qkv: bfloat16 [3, 640, 640], P(None, 'wide', 'narrow'), may hold values from -0.25 to 0.25
- qv_bias: bfloat16 [2, 640], P(None, 'narrow'), may hold values from -1 to 1
- w_out: bfloat16 [640, 640], P('narrow', 'wide'), may hold values from -1.25 to 1.25
- out_bias: bfloat16 [640], P('narrow'), may hold values from -3 to 3
- ln2_gain: bfloat16 [640], P('narrow'), may hold values from 0.25 to 1.75
- ln2_shift: bfloat16 [640], P('narrow'), may hold values from -3 to 3
- w_up: bfloat16 [640, 5120], P('narrow', 'wide'), may hold values from -0.25 to 0.25
- up_bias: bfloat16 [5120], P('wide'), may hold values from -3 to 3
- w_down: bfloat16 [5120, 640], P('wide', 'narrow'), may hold values from -0.078125 to 0.078125
- down_bias: bfloat16 [640], P('narrow'), may hold values from -3 to 3
- segment_ids: int32 [24576], P('wide'), may hold values from 0 to 191, never falling along the last dimension, each value on 1 to 256 neighbouring positions
- out_grad: bfloat16 [640, 24576], P('narrow', 'wide'), may hold values from -6 to 6
- predicted: int32 [24576], P('wide'), may hold values from 0 to 3
- labels: int32 [24576], P('wide'), may hold values from 0 to 4
Outputs:
- layer_out: bfloat16 [640, 24576], P('narrow', 'wide')
- tokens_grad: float32 [640, 24576], P('narrow', 'wide')
- ln1_gain_grad: float32 [640], P('narrow')
- ln1_shift_grad: float32 [640], P('narrow')
- w_qkv_grad: float32 [3, 640, 640], P(None, 'wide', 'narrow')
- qv_bias_grad: float32 [2, 640], P(None, 'narrow')
- w_out_grad: float32 [640, 640], P('narrow', 'wide')
- out_bias_grad: float32 [640], P('narrow')
- ln2_gain_grad: float32 [640], P('narrow')
- ln2_shift_grad: float32 [640], P('narrow')
- w_up_grad: float32 [640, 5120], P('narrow', 'wide')
- up_bias_grad: float32 [5120], P('wide')
- w_down_grad: float32 [5120, 640], P('wide', 'narrow')
- down_bias_grad: float32 [640], P('narrow')
- tallies: int32 [2, 4], replicated
- accuracy: float32 [], replicated
Inputs may be any that keep to these rules, and one draw needn't show every extreme that they name: `segment_ids`: segment numbers never fall along the tokens, and one segment holds at most 256 tokens. `labels`: the value 4 marks a token that is not scored.
All inputs are finite; a program needn't handle non-finite values.
Results may differ from a plain program's by a relative error of at most 0.012.
Values may be sent and summed in bfloat16 or wider, within the bound.
No kernel may reach another device: no remote copies, remote signals or barrier semaphores. Data moves between devices by JAX's collectives and lax.ppermute only.
A program may use at most 256 MiB of HBM per device.

v0:
```python
import jax
import jax.numpy as jnp
from jax import lax
from jax.sharding import PartitionSpec as P

HEAD_DIM = 32
SEQ = 1024
CLASSES = 4


EPS = 1e-05
ROWS_DIMS = (((0,), (0,)), ((), ()))
COLS_DIMS = (((1,), (1,)), ((), ()))


def layer_norm(inputs, gain_vec, shift_vec):
    centre = jnp.mean(inputs, axis=-1, keepdims=True)
    spread = jnp.mean(jnp.square(inputs - centre), axis=-1, keepdims=True)
    return (inputs - centre) * lax.rsqrt(spread + EPS) * gain_vec + shift_vec


def exact_gelu(inputs):
    return jax.nn.gelu(inputs, approximate=False)


def score_block(queries, key_rows, segments):
    raw_scores = jnp.einsum("qhd,khd->hqk", queries, key_rows, preferred_element_type=jnp.float32)
    scaled = raw_scores * queries.shape[-1] ** (-0.5)
    same_doc = segments[:, None] == segments[None, :]
    return jnp.where(same_doc[None], scaled, -1e30)


def attend_forward(block_in):
    queries, key_rows, value_rows, segments = block_in
    scores = score_block(queries, key_rows, segments)
    top_score = jnp.max(scores, axis=-1, keepdims=True)
    exp_scores = jnp.exp(scores - top_score)
    totals = jnp.sum(exp_scores, axis=-1, keepdims=True)
    attn_probs = (exp_scores / totals).astype(jnp.bfloat16)
    attended = jnp.einsum(
        "hqk,khd->qhd", attn_probs, value_rows, preferred_element_type=jnp.float32
    )
    return (attended.astype(jnp.bfloat16), (top_score + jnp.log(totals))[..., 0])


def attend_backward(block_in):
    queries, key_rows, value_rows, segments, log_total, grad_out = block_in
    scores = score_block(queries, key_rows, segments)
    probs_full = jnp.exp(scores - log_total[..., None])
    attn_probs = probs_full.astype(jnp.bfloat16)
    grad_values = jnp.einsum(
        "hqk,qhd->khd", attn_probs, grad_out, preferred_element_type=jnp.float32
    ).astype(jnp.bfloat16)
    grad_probs = jnp.einsum(
        "qhd,khd->hqk", grad_out, value_rows, preferred_element_type=jnp.float32
    )
    inner = jnp.sum(probs_full * grad_probs, axis=-1, keepdims=True)
    grad_scores = (probs_full * (grad_probs - inner) * queries.shape[-1] ** (-0.5)).astype(
        jnp.bfloat16
    )
    grad_queries = jnp.einsum(
        "hqk,khd->qhd", grad_scores, key_rows, preferred_element_type=jnp.float32
    ).astype(jnp.bfloat16)
    grad_keys = jnp.einsum(
        "hqk,qhd->khd", grad_scores, queries, preferred_element_type=jnp.float32
    ).astype(jnp.bfloat16)
    return (grad_queries, grad_keys, grad_values)


def shards(
    tokens_in,
    ln1_gain,
    ln1_shift,
    w_qkv,
    qv_bias,
    w_out,
    out_bias,
    ln2_gain,
    ln2_shift,
    w_up,
    up_bias,
    w_down,
    down_bias,
    segment_ids,
    out_grad,
    predicted,
    labels,
):
    narrow_count = lax.axis_size("narrow")
    my_part = lax.axis_index("narrow")
    width_part, tok_rows = tokens_in.shape
    quarter = tok_rows // narrow_count
    start_row = my_part * quarter
    whole_cols, gain_one, shift_one, bias_out, gain_two, shift_two, bias_down = (
        lax.all_gather(tokens_in, "narrow", axis=0, tiled=True),
        lax.all_gather(ln1_gain, "narrow", axis=0, tiled=True),
        lax.all_gather(ln1_shift, "narrow", axis=0, tiled=True),
        lax.all_gather(out_bias, "narrow", axis=0, tiled=True),
        lax.all_gather(ln2_gain, "narrow", axis=0, tiled=True),
        lax.all_gather(ln2_shift, "narrow", axis=0, tiled=True),
        lax.all_gather(down_bias, "narrow", axis=0, tiled=True),
    )
    qkv_whole, out_whole, up_piece, down_piece, up_bias_whole = (
        lax.all_gather(w_qkv, "wide", axis=1, tiled=True),
        lax.all_gather(w_out, "wide", axis=1, tiled=True),
        lax.all_gather(w_up, "wide", axis=1, tiled=True),
        lax.all_gather(w_down, "wide", axis=0, tiled=True),
        lax.all_gather(up_bias, "wide", axis=0, tiled=True),
    )
    up_whole, down_whole = (
        lax.all_gather(up_piece, "narrow", axis=0, tiled=True),
        lax.all_gather(down_piece, "narrow", axis=1, tiled=True),
    )
    grad_cols_in = lax.all_to_all(out_grad, "narrow", split_axis=1, concat_axis=0, tiled=True)
    grad_rows = grad_cols_in.T
    inputs_full = whole_cols.T.astype(jnp.float32)
    normed_full, norm_one_back = jax.vjp(
        layer_norm, inputs_full, gain_one.astype(jnp.float32), shift_one.astype(jnp.float32)
    )
    normed = normed_full.astype(jnp.bfloat16)
    projected = jnp.einsum("td,cde->cte", normed, qkv_whole, preferred_element_type=jnp.float32)
    bias_pair = qv_bias.astype(jnp.float32)
    queries = (projected[0] + bias_pair[0]).astype(jnp.bfloat16)
    key_rows = projected[1].astype(jnp.bfloat16)
    value_rows = (projected[2] + bias_pair[1]).astype(jnp.bfloat16)
    heads_here = width_part // HEAD_DIM
    seq_count = tok_rows // SEQ
    grid_shape = (seq_count, SEQ, heads_here, HEAD_DIM)
    seg_grid = segment_ids.reshape(seq_count, SEQ)
    query_grid = queries.reshape(grid_shape)
    key_grid = key_rows.reshape(grid_shape)
    value_grid = value_rows.reshape(grid_shape)
    attended, log_total = lax.map(attend_forward, (query_grid, key_grid, value_grid, seg_grid))
    attended = attended.reshape(tok_rows, width_part)
    branch_part = jnp.dot(attended, out_whole, preferred_element_type=jnp.float32)
    branch_sum = lax.psum(branch_part, "narrow")
    middle = inputs_full + (branch_sum + bias_out.astype(jnp.float32))
    middle_cols = lax.dynamic_slice_in_dim(middle, my_part * width_part, width_part, 1)
    middle_rows = lax.dynamic_slice_in_dim(middle, start_row, quarter, 0)
    normed_two_full, norm_two_back = jax.vjp(
        layer_norm, middle_rows, gain_two.astype(jnp.float32), shift_two.astype(jnp.float32)
    )
    normed_two = normed_two_full.astype(jnp.bfloat16)
    hidden = jnp.dot(
        normed_two, up_whole, preferred_element_type=jnp.float32
    ) + up_bias_whole.astype(jnp.float32)
    activated, gelu_back = jax.vjp(exact_gelu, hidden)
    act_low = activated.astype(jnp.bfloat16)
    ffn_rows = jnp.dot(act_low, down_whole, preferred_element_type=jnp.float32) + bias_down.astype(
        jnp.float32
    )
    ffn_cols = lax.all_to_all(
        ffn_rows.T.astype(jnp.bfloat16), "narrow", split_axis=0, concat_axis=1, tiled=True
    ).astype(jnp.float32)
    layer_out = (middle_cols.T + ffn_cols).astype(jnp.bfloat16)
    grad_act = lax.dot_general(grad_rows, down_whole, COLS_DIMS, preferred_element_type=jnp.float32)
    down_grad_full = lax.dot_general(
        act_low, grad_rows, ROWS_DIMS, preferred_element_type=jnp.float32
    )
    grad_hidden = gelu_back(grad_act)[0].astype(jnp.bfloat16)
    up_grad_full = lax.dot_general(
        normed_two, grad_hidden, ROWS_DIMS, preferred_element_type=jnp.float32
    )
    up_bias_part = jnp.sum(grad_hidden, axis=0, dtype=jnp.float32)
    grad_normed_two = lax.dot_general(
        grad_hidden, up_whole, COLS_DIMS, preferred_element_type=jnp.float32
    )
    grad_mid_norm, gain_two_grad, shift_two_grad = norm_two_back(grad_normed_two)
    grad_mid = grad_rows.astype(jnp.float32) + grad_mid_norm
    grad_branch = grad_mid.astype(jnp.bfloat16)
    down_bias_part = jnp.sum(grad_rows, axis=0, dtype=jnp.float32)
    out_bias_part = jnp.sum(grad_branch, axis=0, dtype=jnp.float32)
    branch_whole = lax.all_gather(grad_branch, "narrow", axis=0, tiled=True)
    out_grad_part = lax.dot_general(
        attended, branch_whole, ROWS_DIMS, preferred_element_type=jnp.float32
    )
    grad_attended = lax.dot_general(
        branch_whole, out_whole, COLS_DIMS, preferred_element_type=jnp.float32
    ).astype(jnp.bfloat16)
    grad_queries, grad_keys, grad_values = lax.map(
        attend_backward,
        (query_grid, key_grid, value_grid, seg_grid, log_total, grad_attended.reshape(grid_shape)),
    )
    grad_qkv = jnp.stack(
        [
            grad_queries.reshape(tok_rows, width_part),
            grad_keys.reshape(tok_rows, width_part),
            grad_values.reshape(tok_rows, width_part),
        ]
    )
    qkv_grad_part = jnp.einsum("td,cte->cde", normed, grad_qkv, preferred_element_type=jnp.float32)
    grad_normed = jnp.einsum("cte,cde->td", grad_qkv, qkv_whole, preferred_element_type=jnp.float32)
    grad_in_norm, gain_one_grad, shift_one_grad = norm_one_back(grad_normed)
    own_rows = lax.dynamic_slice_in_dim(grad_in_norm, start_row, quarter, 0) + grad_mid
    residual_term = lax.dynamic_update_slice_in_dim(grad_in_norm, own_rows, start_row, 0)
    vector_rows = jnp.stack(
        [
            gain_one_grad,
            shift_one_grad,
            gain_two_grad,
            shift_two_grad,
            out_bias_part,
            down_bias_part,
        ]
    )
    grad_cols, vector_cols = (
        lax.psum_scatter(residual_term.T, "narrow", scatter_dimension=0, tiled=True),
        lax.psum_scatter(vector_rows, "narrow", scatter_dimension=1, tiled=True),
    )
    bias_grads = jnp.stack(
        [
            jnp.sum(grad_qkv[0], axis=0, dtype=jnp.float32),
            jnp.sum(grad_qkv[2], axis=0, dtype=jnp.float32),
        ]
    )
    class_ids = jnp.arange(CLASSES, dtype=jnp.int32)
    label_hits = labels[:, None] == class_ids
    counts_local = jnp.stack(
        [
            jnp.sum(((predicted[:, None] == class_ids) & label_hits).astype(jnp.float32), axis=0),
            jnp.sum(label_hits.astype(jnp.float32), axis=0),
        ]
    )
    small_sums, count_sums = lax.psum(
        (jnp.concatenate([vector_cols, bias_grads], axis=0), counts_local), "wide"
    )
    qkv_grad, out_weight_grad, up_grad_mid, down_grad_mid, up_bias_grad = (
        lax.psum_scatter(qkv_grad_part, "wide", scatter_dimension=1, tiled=True),
        lax.psum_scatter(out_grad_part, "wide", scatter_dimension=1, tiled=True),
        lax.psum_scatter(up_grad_full, "wide", scatter_dimension=1, tiled=True),
        lax.psum_scatter(down_grad_full, "wide", scatter_dimension=0, tiled=True),
        lax.psum_scatter(up_bias_part, "wide", scatter_dimension=0, tiled=True),
    )
    up_grad, down_grad = (
        lax.psum_scatter(up_grad_mid, "narrow", scatter_dimension=0, tiled=True),
        lax.psum_scatter(down_grad_mid, "narrow", scatter_dimension=1, tiled=True),
    )
    up_bias_grad = lax.psum(up_bias_grad, "narrow")
    tallies = count_sums.astype(jnp.int32)
    accuracy = jnp.sum(count_sums[0]) / jnp.maximum(jnp.sum(count_sums[1]), 1.0)
    return (
        layer_out,
        grad_cols,
        small_sums[0],
        small_sums[1],
        qkv_grad,
        small_sums[6:8],
        out_weight_grad,
        small_sums[4],
        small_sums[2],
        small_sums[3],
        up_grad,
        up_bias_grad,
        down_grad,
        small_sums[5],
        tallies,
        accuracy,
    )


def solution(mesh):
    return jax.shard_map(
        shards,
        mesh=mesh,
        in_specs=(
            P("narrow", "wide"),
            P("narrow"),
            P("narrow"),
            P(None, "wide", "narrow"),
            P(None, "narrow"),
            P("narrow", "wide"),
            P("narrow"),
            P("narrow"),
            P("narrow"),
            P("narrow", "wide"),
            P("wide"),
            P("wide", "narrow"),
            P("narrow"),
            P("wide"),
            P("narrow", "wide"),
            P("wide"),
            P("wide"),
        ),
        out_specs=(
            P("narrow", "wide"),
            P("narrow", "wide"),
            P("narrow"),
            P("narrow"),
            P(None, "wide", "narrow"),
            P(None, "narrow"),
            P("narrow", "wide"),
            P("narrow"),
            P("narrow"),
            P("narrow"),
            P("narrow", "wide"),
            P("wide"),
            P("wide", "narrow"),
            P("narrow"),
            P(),
            P(),
        ),
        check_vma=False,
    )
```

profile of v0, /device:TPU:0, one launch (start us, length us, event | category | flops | bytes accessed | tf_op | source)
XLA Modules:
  0.0 1448.3 jit_solution(14012681986925199467)
XLA Ops:
  17.2 21.8 %all-reduce.8 = (bf16[640]{0:T(1024)(128)(2,1)}, bf16[640]{0:T(1024)(128)(2,1)}, bf16[640]{0:T(1024)(128)(2,1)S(1)}, bf16[640]{0:T(1024)(128)(2,1)S(1)}, bf16[640]{0:T(1024)(128)(2,1)}, /*index=5*/bf16[640]{0:T(1024)(128)(2,1)}) all-reduce(bf16[640]{0:T(1024)(128)(2,1)S(1)} %dynamic-update-slice.4, ...), channel_id=1, replica_groups=mesh['wide'=8,'narrow'=4] {'narrow'}, use_global_device_ids=true, to_apply=%add.4 | all-reduce | flops 3840 | bytes 15360
  52.2 12.6 all_gather.48
  66.0 23.2 %all-gather.8.cloned.1.call-done = bf16[640,3072]{1,0:T(8,128)(2,1)} async-done(((bf16[160,3072]{1,0:T(8,128)(2,1)}), bf16[640,3072]{1,0:T(8,128)(2,1)}) %all-gather.8.cloned.1.call-update) | async-done | bytes 3932176 | tf_op jit(solution)/shard_map/all_gather | solution.py:95
  119.2 51.7 %while.26 = (s32[]{:T(128)}, bf16[3,1024,5,32]{1,3,2,0:T(8,128)(2,1)S(1)}, f32[3,5,1024]{2,1,0:T(8,128)}, bf16[3,1024,5,32]{1,3,2,0:T(8,128)(2,1)S(1)}, s32[3,10...) while((s32[]{:T(128)}, ...), condition=%wide.region_5.6_spmd, body=%wide.region_2.5_spmd.sunk | while | flops 735210496 | bytes 68634728 | solution.py:133
  193.0 40.7 %all-to-all-done.1 = bf16[160,4,768]{2,0,1:T(8,128)(2,1)S(1)} async-done(((bf16[160,4,768]{2,0,1:T(8,128)(2,1)}), bf16[160,4,768]{2,0,1:T(8,128)(2,1)S(1)}, u32[]{:S(2)}, u32[]{:S(2)}) %all-to-all-start.1) | async-done | bytes 983072 | tf_op jit(solution)/shard_map/all_to_all | solution.py:114
  235.1 236.2 %all-reduce.11.cloned.1.call-done = f32[3072,640]{1,0:T(8,128)} async-done(((f32[3072,640]{1,0:T(8,128)}), f32[3072,640]{1,0:T(8,128)}) %all-reduce.11.cloned.1.call-update) | async-done | bytes 7864336 | tf_op jit(solution)/shard_map/psum | solution.py:136
  481.0 110.2 %all-gather.12.cloned.1.call-done = bf16[640,5120]{1,0:T(8,128)(2,1)} async-done(((bf16[160,5120]{1,0:T(8,128)(2,1)}), bf16[640,5120]{1,0:T(8,128)(2,1)}) %all-gather.12.cloned.1.call-update) | async-done | bytes 6553616 | tf_op jit(solution)/shard_map/all_gather | solution.py:111
  591.3 44.5 %multiply_convert_fusion.1 = (bf16[768,5120]{1,0:T(8,128)(2,1)}, f32[768,5120]{1,0:T(8,128)}, f32[768,5120]{1,0:T(8,128)}) fusion(f32[5120]{0:T(1024)S(1)} %bitcast.263, bf16[640,5120]{1,0:T(8,128)(2,1)} %all-gather.12.cloned.1.call-done, f32[640]{0:T(1024)S(1)} %convert_element_type.153, f32[640]{0:T(1024)S(1)} %convert_element_type.152, ...), kind=kOutput, calls=%fused_computation.86 | convolution fusion | flops 5295144960 | bytes 47873028 | tf_op jit(solution)/shard_map/dot_general | solution.py:144
  635.8 74.8 %all-gather.16.cloned.1.call-done = bf16[5120,640]{0,1:T(8,128)(2,1)} async-done(((bf16[5120,160]{0,1:T(8,128)(2,1)}), bf16[5120,640]{0,1:T(8,128)(2,1)}) %all-gather.16.cloned.1.call-update) | async-done | bytes 6553616 | tf_op jit(solution)/shard_map/all_gather | solution.py:112
  710.6 21.8 %convert_reduce_fusion = (f32[5120]{0:T(1024)}, bf16[768,5120]{1,0:T(8,128)(2,1)}) fusion(f32[768,5120]{1,0:T(8,128)} %get-tuple-element.339, bf16[640,768]{1,0:T(8,128)(2,1)S(1)} %bitcast.253, bf16[5120,640]{0,1:T(8,128)(2,1)} %all-gather.16.cloned.1.call-done, f32[768,5120]{1,0:T(8,128)} %get-tuple-element.350, f32[5120]{0:T(1024)S(1)} %bitcast.264), kind=kOutput, calls=%fused_computation.84 | convolution fusion | flops 5100006400 | bytes 46899200 | tf_op jit(solution)/shard_map/dot_general | solution.py:156
  758.1 12.0 fusion.151
  772.8 48.7 %all-gather.18.cloned.1.call-done = bf16[3072,640]{1,0:T(8,128)(2,1)} async-done(((bf16[768,640]{1,0:T(8,128)(2,1)}), bf16[3072,640]{1,0:T(8,128)(2,1)}) %all-gather.18.cloned.1.call-update) | async-done | bytes 3932176 | tf_op jit(solution)/shard_map/all_gather | solution.py:173
  831.1 273.5 %while.27 = (s32[]{:T(128)}, bf16[3,1024,5,32]{1,3,2,0:T(8,128)(2,1)}, bf16[3,1024,5,32]{1,3,2,0:T(8,128)(2,1)}, bf16[3,1024,5,32]{1,3,2,0:T(8,128)(2,1)}, bf16[...) while((s32[]{:T(128)}, ...), condition=%wide.region_14.15_spmd, body=%wide.region_12.14_spmd.sunk | while | flops 1815588864 | bytes 324351136 | solution.py:180
  859.8 32.2 %fusion.208 = bf16[3,1024,5,32]{1,3,2,0:T(8,128)(2,1)} fusion(bf16[3,1024,5,32]{1,3,2,0:T(8,128)(2,1)} %get-tuple-element.502, s32[]{:T(128)S(6)} %copy.201, f32[5,1024,1024]{1,2,0:T(8,128)} %fusion.205, f32[5,1024,1024]{1,2,0:T(8,128)} %copy-done, f32[5,1024]{1,0:T(8,128)S(1)} %dynamic-slice_bitcast_fusion.2, ...), kind=kOutput, calls=%fused_computation.48.clone.1 | convolution fusion | flops 393385984 | bytes 86705152 | tf_op jit(solution)/shard_map/while/body/eval_jaxpr/hqk,qhd->khd/dot_general | solution.py:64
  892.0 31.7 %fusion.207 = bf16[3,1024,5,32]{1,3,2,0:T(8,128)(2,1)} fusion(bf16[3,1024,5,32]{1,3,2,0:T(8,128)(2,1)} %get-tuple-element.501, s32[]{:T(128)S(6)} %copy.201, f32[5,1024,1024]{1,2,0:T(8,128)} %fusion.205, f32[5,1024,1024]{1,2,0:T(8,128)} %copy-done, f32[5,1024]{1,0:T(8,128)S(1)} %dynamic-slice_bitcast_fusion.2, ...), kind=kOutput, calls=%fused_computation.50.clone.1 | convolution fusion | flops 393385984 | bytes 86705152 | tf_op jit(solution)/shard_map/while/body/eval_jaxpr/hqk,khd->qhd/dot_general | solution.py:61
  954.6 32.0 %fusion.208 = bf16[3,1024,5,32]{1,3,2,0:T(8,128)(2,1)} fusion(bf16[3,1024,5,32]{1,3,2,0:T(8,128)(2,1)} %get-tuple-element.502, s32[]{:T(128)S(6)} %copy.201, f32[5,1024,1024]{1,2,0:T(8,128)} %fusion.205, f32[5,1024,1024]{1,2,0:T(8,128)} %copy-done, f32[5,1024]{1,0:T(8,128)S(1)} %dynamic-slice_bitcast_fusion.2, ...), kind=kOutput, calls=%fused_computation.48.clone.1 | convolution fusion | flops 393385984 | bytes 86705152 | tf_op jit(solution)/shard_map/while/body/eval_jaxpr/hqk,qhd->khd/dot_general | solution.py:64
  986.6 31.7 %fusion.207 = bf16[3,1024,5,32]{1,3,2,0:T(8,128)(2,1)} fusion(bf16[3,1024,5,32]{1,3,2,0:T(8,128)(2,1)} %get-tuple-element.501, s32[]{:T(128)S(6)} %copy.201, f32[5,1024,1024]{1,2,0:T(8,128)} %fusion.205, f32[5,1024,1024]{1,2,0:T(8,128)} %copy-done, f32[5,1024]{1,0:T(8,128)S(1)} %dynamic-slice_bitcast_fusion.2, ...), kind=kOutput, calls=%fused_computation.50.clone.1 | convolution fusion | flops 393385984 | bytes 86705152 | tf_op jit(solution)/shard_map/while/body/eval_jaxpr/hqk,khd->qhd/dot_general | solution.py:61
  1044.2 30.2 %fusion.208 = bf16[3,1024,5,32]{1,3,2,0:T(8,128)(2,1)} fusion(bf16[3,1024,5,32]{1,3,2,0:T(8,128)(2,1)} %get-tuple-element.502, s32[]{:T(128)S(6)} %copy.201, f32[5,1024,1024]{1,2,0:T(8,128)} %fusion.205, f32[5,1024,1024]{1,2,0:T(8,128)} %copy-done, f32[5,1024]{1,0:T(8,128)S(1)} %dynamic-slice_bitcast_fusion.2, ...), kind=kOutput, calls=%fused_computation.48.clone.1 | convolution fusion | flops 393385984 | bytes 86705152 | tf_op jit(solution)/shard_map/while/body/eval_jaxpr/hqk,qhd->khd/dot_general | solution.py:64
  1074.4 30.1 %fusion.207 = bf16[3,1024,5,32]{1,3,2,0:T(8,128)(2,1)} fusion(bf16[3,1024,5,32]{1,3,2,0:T(8,128)(2,1)} %get-tuple-element.501, s32[]{:T(128)S(6)} %copy.201, f32[5,1024,1024]{1,2,0:T(8,128)} %fusion.205, f32[5,1024,1024]{1,2,0:T(8,128)} %copy-done, f32[5,1024]{1,0:T(8,128)S(1)} %dynamic-slice_bitcast_fusion.2, ...), kind=kOutput, calls=%fused_computation.50.clone.1 | convolution fusion | flops 393385984 | bytes 86705152 | tf_op jit(solution)/shard_map/while/body/eval_jaxpr/hqk,khd->qhd/dot_general | solution.py:61
  1188.3 23.2 %all-to-all-done = bf16[4,160,768]{2,1,0:T(8,128)(2,1)S(1)} async-done(((bf16[4,160,768]{2,1,0:T(8,128)(2,1)}), bf16[4,160,768]{2,1,0:T(8,128)(2,1)S(1)}, u32[]{:S(2)}, u32[]{:S(2)}) %all-to-all-start) | async-done | bytes 983072 | tf_op jit(solution)/shard_map/all_to_all | solution.py:152
  1225.5 25.0 %all-reduce.7 = (f32[8,160]{1,0:T(8,128)S(1)}, f32[5120]{0:T(1024)S(1)}, f32[2,4]{1,0:T(2,128)S(1)}) all-reduce(f32[8,160]{1,0:T(8,128)S(1)} %pad_maximum_fusion, f32[5120]{0:T(1024)S(1)} %copy-done.26, f32[2,4]{1,0:T(2,128)S(1)} %pad_maximum_fusion.1), channel_id=1, replica_groups=mesh['wide'=8,'narrow'=4] {'wide'}, use_global_device_ids=true, to_apply=%region_28.29 | all-reduce | flops 6408 | bytes 51264 | tf_op jit(solution)/shard_map/psum | solution.py:224
  1268.7 93.9 %reduce-scatter.25.cloned.1.call-done = f32[160,3072]{1,0:T(8,128)} async-done(((f32[640,3072]{1,0:T(8,128)}), f32[160,3072]{1,0:T(8,128)}) %reduce-scatter.25.cloned.1.call-update) | async-done | bytes 1966096
  1362.6 39.6 %reduce-scatter.21.cloned.1.call-done = f32[160,640]{1,0:T(8,128)} async-done(((f32[640,640]{1,0:T(8,128)}), f32[160,640]{1,0:T(8,128)}) %reduce-scatter.21.cloned.1.call-update) | async-done | bytes 409616 | tf_op jit(solution)/shard_map/reduce_scatter | solution.py:235
  1402.2 38.2 %reduce-scatter.33.cloned.1.call-done = f32[160,640]{1,0:T(8,128)} async-done(((f32[640,640]{1,0:T(8,128)}), f32[160,640]{1,0:T(8,128)}) %reduce-scatter.33.cloned.1.call-update) | async-done | bytes 409616
  (288 shorter events, 374.2 us)
Async XLA Ops:
  7.2 81.9 %all-gather.8.cloned.1.call-start = ((), (), s32[]{:S(2)}) async-start(), calls=%async_computation.10 | async-start | bytes 4915200 | tf_op jit(solution)/shard_map/all_gather | solution.py:95
  7.9 170.2 %all-gather.10.cloned.1.call-start = ((), (), s32[]{:S(2)}) async-start(), calls=%async_computation.12 | async-start | bytes 1843200 | tf_op jit(solution)/shard_map/all_gather | solution.py:106
  8.7 226.4 %all-gather.14.cloned.1.call-start = ((), (), s32[]{:S(2)}) async-start(), calls=%async_computation.14 | async-start | bytes 1843200 | tf_op jit(solution)/shard_map/all_gather | solution.py:107
  9.4 461.9 %all-reduce.11.cloned.1.call-start = ((), (), s32[]{:S(2)}) async-start(), calls=%async_computation.11 | async-start | bytes 15728640 | tf_op jit(solution)/shard_map/psum | solution.py:136
  39.0 63.0 %copy-start.27 = (f32[640]{0:T(1024)}, f32[640]{0:T(1024)S(1)}, u32[]{:S(2)}) copy-start(f32[640]{0:T(1024)S(1)} %convert_element_type.144) | copy-start | bytes 7684
  39.0 63.0 %copy-start.35 = (f32[640]{0:T(1024)}, f32[640]{0:T(1024)S(1)}, u32[]{:S(2)}) copy-start(f32[640]{0:T(1024)S(1)} %convert_element_type.145) | copy-start | bytes 7684
  66.0 36.1 %copy-start.15 = (bf16[3,640,160]{1,2,0:T(8,128)(2,1)}, bf16[3,640,160]{1,2,0:T(8,128)(2,1)S(1)}, u32[]{:S(2)}) copy-start(bf16[3,640,160]{1,2,0:T(8,128)(2,1)S(1)} %copy.136) | copy-start | bytes 1843204
  119.2 54.1 %copy-start.12 = (bf16[160,640]{0,1:T(8,128)(2,1)S(1)}, bf16[160,640]{0,1:T(8,128)(2,1)}, u32[]{:S(2)}) copy-start(bf16[160,640]{0,1:T(8,128)(2,1)} %all_gather.49) | copy-start | bytes 614404
  178.0 413.3 %all-gather.12.cloned.1.call-start = ((), (), s32[]{:S(2)}) async-start(), calls=%async_computation.13 | async-start | bytes 8192000 | tf_op jit(solution)/shard_map/all_gather | solution.py:111
  180.2 53.5 %all-to-all-start.1 = ((bf16[160,4,768]{2,0,1:T(8,128)(2,1)}), bf16[160,4,768]{2,0,1:T(8,128)(2,1)S(1)}, u32[]{:S(2)}, u32[]{:S(2)}) async-start(bf16[160,4,768]{2,0,1:T(8,128)(2,1)} %bitcast.208), calls=%async_computation.1 | async-start | bytes 1966080 | tf_op jit(solution)/shard_map/all_to_all | solution.py:114
  183.8 526.8 %all-gather.16.cloned.1.call-start = ((), (), s32[]{:S(2)}) async-start(), calls=%async_computation.15 | async-start | bytes 8192000 | tf_op jit(solution)/shard_map/all_gather | solution.py:112
  233.7 242.8 %copy-start.9 = (bf16[160,4,768]{2,0,1:T(8,128)(2,1)}, bf16[160,4,768]{2,0,1:T(8,128)(2,1)S(1)}, u32[]{:S(2)}) copy-start(bf16[160,4,768]{2,0,1:T(8,128)(2,1)S(1)} %all-to-all-done.1) | copy-start | bytes 2949124
  235.1 586.5 %all-gather.18.cloned.1.call-start = ((), (), s32[]{:S(2)}) async-start(), calls=%async_computation.16 | async-start | bytes 4915200 | tf_op jit(solution)/shard_map/all_gather | solution.py:173
  591.3 119.3 %copy-start.10 = (bf16[160,4,768]{2,0,1:T(8,128)(2,1)S(1)}, bf16[160,4,768]{2,0,1:T(8,128)(2,1)}, u32[]{:S(2)}) copy-start(bf16[160,4,768]{2,0,1:T(8,128)(2,1)} %copy-done.9) | copy-start | bytes 2949124
  746.7 422.7 %reduce-scatter.19.cloned.1.call-start = ((), (), s32[]{:S(2)}) async-start(), calls=%async_computation.17 | async-start | bytes 14745600 | tf_op jit(solution)/shard_map/reduce_scatter | solution.py:230
  758.1 411.9 %reduce-scatter.23.cloned.1.call-start = ((), (), s32[]{:S(2)}) async-start(), calls=%async_computation.19 | async-start | bytes 14745600 | tf_op jit(solution)/shard_map/reduce_scatter | solution.py:231
  770.1 51.4 %copy-start.13 = (bf16[160,640]{0,1:T(8,128)(2,1)S(1)}, bf16[160,640]{0,1:T(8,128)(2,1)}, u32[]{:S(2)}) copy-start(bf16[160,640]{0,1:T(8,128)(2,1)} %all_gather.49) | copy-start | bytes 614404
  770.2 454.3 %reduce-scatter.27.cloned.1.call-start = ((), (), s32[]{:S(2)}) async-start(), calls=%async_computation.21 | async-start | bytes 409600
  1126.7 138.5 %reduce-scatter.31.cloned.1.call-start = ((), (), s32[]{:S(2)}) async-start(), calls=%async_computation.23 | async-start | bytes 737280
  1131.4 135.5 %reduce-scatter.29.cloned.1.call-start = ((), (), s32[]{:S(2)}) async-start(), calls=%async_computation.22 | async-start | bytes 1474560
  1143.8 218.8 %reduce-scatter.25.cloned.1.call-start = ((), (), s32[]{:S(2)}) async-start(), calls=%async_computation.20 | async-start | bytes 9830400
  1169.3 232.9 %reduce-scatter.21.cloned.1.call-start = ((), (), s32[]{:S(2)}) async-start(), calls=%async_computation.18 | async-start | bytes 2048000 | tf_op jit(solution)/shard_map/reduce_scatter | solution.py:235
  1169.9 270.5 %reduce-scatter.33.cloned.1.call-start = ((), (), s32[]{:S(2)}) async-start(), calls=%async_computation.24 | async-start | bytes 2048000
  1183.3 28.2 %all-to-all-start = ((bf16[4,160,768]{2,1,0:T(8,128)(2,1)}), bf16[4,160,768]{2,1,0:T(8,128)(2,1)S(1)}, u32[]{:S(2)}, u32[]{:S(2)}) async-start(bf16[4,160,768]{2,1,0:T(8,128)(2,1)} %bitcast.29), calls=%async_computation | async-start | bytes 1966080 | tf_op jit(solution)/shard_map/all_to_all | solution.py:152
  (38 other events, 300.3 us)
Sparse Core Ops, SparseCore 0:
  9.6 79.4 all-gather.7
  91.0 24.6 all-gather.9
  117.6 26.0 all-gather.13
  178.1 293.1 all-reduce.10
  472.7 118.5 all-gather.11
  592.7 117.8 all-gather.15
  746.8 74.6 all-gather.17
  825.1 93.7 reduce-scatter.18
  922.5 95.1 reduce-scatter.22
  1126.8 19.8 reduce-scatter.26
  1149.9 32.8 reduce-scatter.30
  1185.9 37.2 reduce-scatter.28
  1226.1 136.4 reduce-scatter.24
  1365.3 36.7 reduce-scatter.20
  1405.0 35.3 reduce-scatter.32
where the time goes:
time: 1450 us
  waiting for transfers between devices  732 us (50%)
  matrix products  438 us (30%)
  local copies, waits for them, and re-layouts  95.1 us (7%)
  blocking collectives  89.9 us (6%)
  other arithmetic  65.8 us (5%)
  between operations  18.8 us (1%)
    psum x1, waiting for transfers between devices, shards(): branch_sum = lax.psum(branch_part, 'narrow')  236 us
    unnamed x20, waiting for transfers between devices  135 us
    all_gather x1, waiting for transfers between devices, shards(): lax.all_gather(up_piece, 'narrow', axis=0, tiled=True)  110 us
    dot_general x3, matrix products, attend_backward(): jnp.einsum('hqk,qhd->khd', grad_scores, queries, preferred_element_type=j...  94.4 us
    dot_general x3, matrix products, attend_backward(): jnp.einsum('hqk,khd->qhd', grad_scores, key_rows, preferred_element_type=...  93.5 us
    all_gather x1, waiting for transfers between devices, shards(): lax.all_gather(down_piece, 'narrow', axis=1, tiled=True)  74.8 us
    all_gather x1, waiting for transfers between devices, shards(): branch_whole = lax.all_gather(grad_branch, 'narrow', axis=0, tiled=True)  48.7 us
    dot_general x1, matrix products, shards(): jnp.dot(normed_two, up_whole, preferred_element_type=jnp.float32)  44.5 us
  transfers between devices with their start and end apart: 17, of which 10 were waited for; matrix products, arithmetic and copies ran while one was open for 38% of the time, Pallas kernels for 0%

commit v1 on v0

v1 whole, which is shorter than its diff:
```python
import functools

import jax
import jax.numpy as jnp
from jax import lax
from jax.experimental import pallas as pl
from jax.experimental.pallas import tpu as pltpu
from jax.sharding import PartitionSpec as P

HEAD_DIM = 32
SEQ = 1024
CLASSES = 4
LONGEST = 256
EPS = 1e-05
QT = 256
KT = 128
GROUP = 4
LANES = 128
LOG2E = 1.4426950408889634
SCALE = HEAD_DIM**-0.5
MASKED = -1e30
VMEM_LIMIT = 56 * 1024 * 1024
bf16, f32 = jnp.bfloat16, jnp.float32

NN = (((1,), (0,)), ((), ()))
NT = (((1,), (1,)), ((), ()))
TN = (((0,), (0,)), ((), ()))

PHI_P = 0.33
PHI_C = (
    0.1328227541618569,
    0.117797452145417,
    0.18652846971894854,
    -0.09893620415601319,
    0.3406397450924515,
    -0.22542553879715763,
    0.046573313873415075,
)


def mm(left, right, dims=NN):
    return lax.dot_general(left, right, dims, preferred_element_type=f32)


def normal_cdf(u):
    bell = jnp.exp(-0.5 * (u * u))
    t = 1.0 / (1.0 + PHI_P * jnp.abs(u))
    tail = jnp.full_like(t, PHI_C[-1])
    for c in PHI_C[-2::-1]:
        tail = tail * t + c
    tail = tail * t * bell
    return jnp.where(u >= 0, 1.0 - tail, tail), bell * 0.3989422804014327


def head_only(block, h, axis):
    index = lax.broadcasted_iota(jnp.int32, block.shape, axis)
    keep = (index >= h * HEAD_DIM) & (index < (h + 1) * HEAD_DIM)
    return jnp.where(keep, block, jnp.zeros_like(block))


def key_bias(segk_ref, segq_ref, start, window):
    segk = segk_ref[pl.ds(start, window), :]
    segk = jnp.concatenate([segk] * (QT // LANES), axis=1)
    return jnp.where(segk == segq_ref[0:1, :], 0.0, MASKED).astype(f32)


def attend_forward(start_ref, small_ref, q_ref, k_ref, vt_ref, segk_ref, segq_ref, att_ref, lse_ref):
    tile = pl.program_id(1)

    def run(window):
        start = pl.multiple_of(start_ref[tile] * KT, KT)
        keys = k_ref[pl.ds(start, window), :]
        bias = key_bias(segk_ref, segq_ref, start, window)
        q = q_ref[...]
        for h in range(GROUP):
            rows = slice(h * HEAD_DIM, (h + 1) * HEAD_DIM)
            scores = mm(keys, head_only(q, h, 0)) + bias
            top = jnp.max(scores, axis=0, keepdims=True)
            probs = jnp.exp2((scores - top) * (SCALE * LOG2E))
            total = jnp.sum(probs, axis=0, keepdims=True)
            out = mm(vt_ref[rows, pl.ds(start, window)], probs.astype(bf16))
            att_ref[rows, :] = (out / total).astype(bf16)
            lse_ref[h : h + 1, :] = top * (SCALE * LOG2E) + jnp.log2(total)

    @pl.when(small_ref[tile] == 1)
    def _():
        run(4 * KT)

    @pl.when(small_ref[tile] == 0)
    def _():
        run(6 * KT)


def attend_backward(
    start_ref, small_ref, qt_ref, q_ref, kt_ref, k_ref, v_ref, dot_ref, do_ref, att_ref, lse_ref,
    segk_ref, segq_ref, dqt_ref, dk_ref, dv_ref, dk_sum, dv_sum,
):
    tile = pl.program_id(1)

    @pl.when(tile == 0)
    def _():
        dk_sum[...] = jnp.zeros_like(dk_sum)
        dv_sum[...] = jnp.zeros_like(dv_sum)

    def run(window):
        start = pl.multiple_of(start_ref[tile] * KT, KT)
        at = pl.ds(start, window)
        keys, values = k_ref[at, :], v_ref[at, :]
        bias = key_bias(segk_ref, segq_ref, start, window)
        qt, q, dot, do = qt_ref[...], q_ref[...], dot_ref[...], do_ref[...]
        inner = dot.astype(f32) * att_ref[...].astype(f32)
        dk = jnp.zeros((window, LANES), f32)
        dv = jnp.zeros((window, LANES), f32)
        for h in range(GROUP):
            rows = slice(h * HEAD_DIM, (h + 1) * HEAD_DIM)
            delta = jnp.sum(inner[rows, :], axis=0, keepdims=True)
            scores = mm(keys, head_only(qt, h, 0)) * (SCALE * LOG2E)
            probs = jnp.exp2((scores - lse_ref[h : h + 1, :]) + bias)
            dv = dv + mm(probs.astype(bf16), head_only(do, h, 1))
            grad_probs = mm(values, head_only(dot, h, 0))
            grad_scores = (probs * (grad_probs - delta)).astype(bf16)
            dk = dk + mm(grad_scores, head_only(q, h, 1))
            dq = mm(kt_ref[rows, at], grad_scores)
            dqt_ref[rows, :] = (dq * SCALE).astype(bf16)
        dk_sum[at, :] += dk
        dv_sum[at, :] += dv

    @pl.when(small_ref[tile] == 1)
    def _():
        run(4 * KT)

    @pl.when(small_ref[tile] == 0)
    def _():
        run(6 * KT)

    @pl.when(tile == pl.num_programs(1) - 1)
    def _():
        dk_ref[...] = (dk_sum[...] * SCALE).astype(bf16)
        dv_ref[...] = dv_sum[...].astype(bf16)


def attention_specs(span, D):
    spec = pl.BlockSpec
    return {
        "q_cols": spec((LANES, QT), lambda g, j, *_: (g, j)),
        "q_rows": spec((QT, LANES), lambda g, j, *_: (j, g)),
        "k_cols": spec((LANES, span), lambda g, j, *_: (g, 0)),
        "k_rows": spec((span, LANES), lambda g, j, *_: (0, g)),
        "lse": spec((8, QT), lambda g, j, *_: (g, j)),
        "segk": spec((span, LANES), lambda g, j, *_: (0, 0)),
        "segq": spec((8, QT), lambda g, j, *_: (0, j)),
    }


def run_forward(starts, small, qt, k, vt, segk, segq):
    D, rows = qt.shape
    span = k.shape[0]
    s = attention_specs(span, D)
    groups = D // LANES
    return pl.pallas_call(
        attend_forward,
        grid_spec=pltpu.PrefetchScalarGridSpec(
            num_scalar_prefetch=2,
            grid=(groups, rows // QT),
            in_specs=[s["q_cols"], s["k_rows"], s["k_cols"], s["segk"], s["segq"]],
            out_specs=[s["q_cols"], s["lse"]],
        ),
        out_shape=[
            jax.ShapeDtypeStruct((D, rows), bf16),
            jax.ShapeDtypeStruct((groups * 8, rows), f32),
        ],
        compiler_params=pltpu.CompilerParams(vmem_limit_bytes=VMEM_LIMIT),
        cost_estimate=pl.CostEstimate(flops=2 * 10**10, bytes_accessed=10**7, transcendentals=10**7),
        name="attend_forward",
    )(starts, small, qt, k, vt, segk, segq)


def run_backward(starts, small, qt, q, kt, k, v, dot, do, att, lse, segk, segq):
    D, rows = qt.shape
    span = k.shape[0]
    s = attention_specs(span, D)
    return pl.pallas_call(
        attend_backward,
        grid_spec=pltpu.PrefetchScalarGridSpec(
            num_scalar_prefetch=2,
            grid=(D // LANES, rows // QT),
            in_specs=[
                s["q_cols"], s["q_rows"], s["k_cols"], s["k_rows"], s["k_rows"], s["q_cols"], s["q_rows"],
                s["q_cols"], s["lse"], s["segk"], s["segq"],
            ],
            out_specs=[s["q_cols"], s["k_rows"], s["k_rows"]],
            scratch_shapes=[pltpu.VMEM((span, LANES), f32), pltpu.VMEM((span, LANES), f32)],
        ),
        out_shape=[
            jax.ShapeDtypeStruct((D, rows), bf16),
            jax.ShapeDtypeStruct((span, D), bf16),
            jax.ShapeDtypeStruct((span, D), bf16),
        ],
        compiler_params=pltpu.CompilerParams(vmem_limit_bytes=VMEM_LIMIT),
        cost_estimate=pl.CostEstimate(flops=4 * 10**10, bytes_accessed=2 * 10**7, transcendentals=10**7),
        name="attend_backward",
    )(starts, small, qt, q, kt, k, v, dot, do, att, lse, segk, segq)


def feed_forward(first, *refs):
    n2_ref, g_ref, up_ref, dt_ref, ub_ref = refs[:5]
    refs = refs[5:]
    if not first:
        out_in, gn_in = refs[:2]
        refs = refs[2:]
    out_ref, gn_ref, dup_ref, ddt_ref, dub_ref, up_t, down, dup_sum, ddt_sum = refs
    step = pl.program_id(0) * pl.num_programs(1) + pl.program_id(1)
    last = pl.num_programs(0) * pl.num_programs(1) - 1

    @pl.when(step == 0)
    def _():
        up_t[...] = up_ref[...].T
        down[...] = dt_ref[...].T
        dup_sum[...] = jnp.zeros_like(dup_sum)
        ddt_sum[...] = jnp.zeros_like(ddt_sum)
        dub_ref[...] = jnp.zeros_like(dub_ref)

    n2, g = n2_ref[0], g_ref[0]
    hidden = mm(up_t[...], n2) + ub_ref[...]
    grad_act = mm(down[...], g)
    cdf, pdf = normal_cdf(hidden)
    act = (hidden * cdf).astype(bf16)
    grad_hidden = (grad_act * (cdf + hidden * pdf)).astype(bf16)
    out = mm(dt_ref[...], act)
    gn = mm(up_ref[...], grad_hidden)
    if first:
        out_ref[0], gn_ref[0] = out, gn
    else:
        out_ref[0] = out_in[0] + out
        gn_ref[0] = gn_in[0] + gn
    dup_sum[...] += mm(n2, grad_hidden, NT)
    ddt_sum[...] += mm(g, act, NT)
    wide_sum = grad_hidden.astype(f32)
    dub_ref[...] += sum(wide_sum[:, i : i + LANES] for i in range(0, wide_sum.shape[1], LANES))

    @pl.when(step == last)
    def _():
        dup_ref[...] = dup_sum[...].astype(bf16)
        ddt_ref[...] = ddt_sum[...].astype(bf16)


def run_feed_forward(n2, g, up, dt, ub, sums):
    pair, D, rows = n2.shape
    F = up.shape[1]
    tile = QT
    first = sums is None
    whole = lambda shape: pl.BlockSpec(shape, lambda i, j: (0,) * len(shape))
    cols = pl.BlockSpec((1, D, tile), lambda i, j: (i, 0, j))
    sums = () if first else tuple(sums)
    return pl.pallas_call(
        functools.partial(feed_forward, first),
        grid=(pair, rows // tile),
        in_specs=[cols, cols, whole((D, F)), whole((D, F)), whole((F, 1))] + [cols] * len(sums),
        out_specs=[cols, cols, whole((D, F)), whole((D, F)), whole((F, LANES))],
        out_shape=[
            jax.ShapeDtypeStruct((pair, D, rows), f32),
            jax.ShapeDtypeStruct((pair, D, rows), f32),
            jax.ShapeDtypeStruct((D, F), bf16),
            jax.ShapeDtypeStruct((D, F), bf16),
            jax.ShapeDtypeStruct((F, LANES), f32),
        ],
        scratch_shapes=[
            pltpu.VMEM((F, D), bf16),
            pltpu.VMEM((F, D), bf16),
            pltpu.VMEM((D, F), f32),
            pltpu.VMEM((D, F), f32),
        ],
        input_output_aliases={} if first else {5: 0, 6: 1},
        compiler_params=pltpu.CompilerParams(vmem_limit_bytes=VMEM_LIMIT),
        cost_estimate=pl.CostEstimate(
            flops=12 * pair * rows * D * F, bytes_accessed=2 * 10**7, transcendentals=10**6
        ),
        name="feed_forward",
    )(n2, g, up, dt, ub, *sums)


def norm_parts(cols):
    centre = jnp.mean(cols, axis=0, keepdims=True)
    shifted = cols - centre
    spread = jnp.mean(jnp.square(shifted), axis=0, keepdims=True)
    scale = lax.rsqrt(spread + EPS)
    return shifted * scale, scale


def norm_back(grad, xhat, scale, gain):
    e = grad * gain
    mean_e = jnp.mean(e, axis=0, keepdims=True)
    mean_ex = jnp.mean(e * xhat, axis=0, keepdims=True)
    return scale * (e - mean_e - xhat * mean_ex)


def z_rotate(x, k):
    n = lax.axis_size("narrow")
    return lax.ppermute(x, "narrow", [(i, (i + k) % n) for i in range(n)])


def z_gather(x):
    n, me = lax.axis_size("narrow"), lax.axis_index("narrow")
    stack = jnp.stack([x] + [z_rotate(x, k) for k in range(1, n)])
    return [lax.dynamic_index_in_dim(stack, lax.rem(me - j + n, n), 0, False) for j in range(n)]


def z_scatter_sum(pieces):
    n, me = lax.axis_size("narrow"), lax.axis_index("narrow")
    total = lax.dynamic_index_in_dim(pieces, me, 0, False).astype(f32)
    for k in range(1, n):
        piece = lax.dynamic_index_in_dim(pieces, lax.rem(me + k, n), 0, False)
        total = total + z_rotate(piece, k).astype(f32)
    return total


def swap(x, mask):
    n = lax.axis_size("wide")
    return lax.ppermute(x, "wide", [(i, i ^ mask) for i in range(n)])


def wide_sum(x):
    bit = 1
    while bit < lax.axis_size("wide"):
        x = x + swap(x, bit)
        bit *= 2
    return x


CORE, X, Y = 1, 2, 4


def high_bits():
    bits, bit = [], 8
    while bit < lax.axis_size("wide"):
        bits.append(bit)
        bit *= 2
    return bits


def shards(
    tokens_in,
    ln1_gain,
    ln1_shift,
    w_qkv,
    qv_bias,
    w_out,
    out_bias,
    ln2_gain,
    ln2_shift,
    w_up,
    up_bias,
    w_down,
    down_bias,
    segment_ids,
    out_grad,
    predicted,
    labels,
):
    nn, me = lax.axis_size("narrow"), lax.axis_index("narrow")
    nw, mw = lax.axis_size("wide"), lax.axis_index("wide")
    part, tok = tokens_in.shape
    D = part * nn
    quarter = tok // nn
    halo = LONGEST
    span = quarter + 2 * halo
    high = high_bits()

    padded = jnp.pad(tokens_in, ((0, 0), (halo, halo)))
    blocks = jnp.stack([padded[:, j * quarter : j * quarter + span] for j in range(nn)])
    x_low = lax.all_to_all(blocks, "narrow", 0, 0, tiled=True).reshape(D, span)

    vectors = jnp.stack(
        [ln1_gain, ln1_shift, qv_bias[0], qv_bias[1], out_bias, ln2_gain, ln2_shift, down_bias]
    )
    vectors = jnp.concatenate(z_gather(vectors), axis=1).astype(f32)[:, :, None]
    gain_one, shift_one, q_bias, v_bias, bias_out, gain_two, shift_two, bias_down = vectors

    dw = w_qkv.shape[1]
    attn_piece = jnp.concatenate([w_qkv, w_out.T[None]], axis=0)
    attn_own = jnp.concatenate(z_gather(attn_piece), axis=2)[None]
    order = [0]
    for bit in high:
        attn_own = jnp.concatenate([attn_own, swap(attn_own, bit)], axis=0)
        order = order + [m ^ bit for m in order]
    from_x, from_y = swap(attn_own, X), swap(attn_own, Y)
    from_xy = jnp.concatenate([swap(from_y[:, :2], X), swap(from_x[:, 2:], Y)], axis=1)
    attn_half = jnp.concatenate([attn_own, from_x, from_y, from_xy], axis=0)
    order = [m ^ b for b in (0, X, Y, X | Y) for m in order]
    attn_all = jnp.concatenate([attn_half, swap(attn_half, CORE)], axis=0)
    order = order + [m ^ CORE for m in order]
    place = jnp.array([order.index(m) for m in range(nw)], jnp.int32)
    attn_all = jnp.concatenate(
        [lax.dynamic_index_in_dim(attn_all, place[mw ^ w], 0, True) for w in range(nw)], axis=0
    )
    attn_whole = attn_all.transpose(1, 0, 2, 3).reshape(4, D, D)
    wq, wk, wv, wo_t = attn_whole

    up_own = jnp.concatenate(z_gather(w_up), axis=0)
    dt_own = jnp.concatenate(z_gather(w_down.T), axis=0)
    ub_own = up_bias.astype(f32)[None]
    for bit in high:
        up_own = jnp.concatenate([up_own, swap(up_own, bit)], axis=1)
        dt_own = jnp.concatenate([dt_own, swap(dt_own, bit)], axis=1)
        ub_own = jnp.concatenate([ub_own, swap(ub_own, bit)], axis=1)
    up_x, dt_x, up_y, dt_y = swap(up_own, X), swap(dt_own, X), swap(up_own, Y), swap(dt_own, Y)
    up_xy, dt_xy = swap(up_y, X), swap(dt_x, Y)
    ub_x, ub_y, ub_xy = swap(ub_own, X), swap(ub_own, Y), swap(ub_own, X | Y)

    grad_blocks = jnp.stack([out_grad[:, j * quarter : (j + 1) * quarter] for j in range(nn)])
    grad_cols = lax.all_to_all(grad_blocks, "narrow", 0, 0, tiled=True).reshape(D, quarter)
    grad_pair = jnp.stack([grad_cols, swap(grad_cols, CORE)])

    position = jnp.arange(tok, dtype=jnp.int32)
    chunk = segment_ids * (tok // SEQ) + position // SEQ
    big = jnp.int32(2**30)
    chunk = jnp.concatenate([jnp.full((halo,), -1, jnp.int32), chunk, jnp.full((halo,), big, jnp.int32)])
    chunk = lax.dynamic_slice_in_dim(chunk, me * quarter, span, 0)
    chunk_own = chunk[halo : halo + quarter]
    tiles = quarter // QT
    edges = chunk_own.reshape(tiles, QT)
    low = jnp.sum((chunk[None] < edges[:, :1]).astype(jnp.int32), axis=1) // KT
    top = (jnp.sum((chunk[None] <= edges[:, -1:]).astype(jnp.int32), axis=1) + KT - 1) // KT
    small = (top - low <= 4).astype(jnp.int32)
    starts = jnp.minimum(low, span // KT - jnp.where(small == 1, 4, 6))
    segk = jnp.broadcast_to(chunk[:, None], (span, LANES))
    segq = jnp.broadcast_to(chunk_own[None], (8, quarter))

    x_cols = x_low.astype(f32)
    xhat_one, scale_one = norm_parts(x_cols)
    normed = (xhat_one * gain_one + shift_one).astype(bf16)
    own = slice(halo, halo + quarter)
    normed_own = normed[:, own]
    qt = (mm(wq, normed_own, TN) + q_bias).astype(bf16)
    kt = mm(wk, normed, TN).astype(bf16)
    vt = (mm(wv, normed, TN) + v_bias).astype(bf16)
    q, k, v = qt.T, kt.T, vt.T
    att, lse = run_forward(starts, small, qt, k, vt, segk, segq)
    branch = mm(wo_t, att)
    middle = x_cols[:, own] + (branch + bias_out)
    xhat_two, scale_two = norm_parts(middle)
    normed_two = (xhat_two * gain_two + shift_two).astype(bf16)

    pair = jnp.stack([normed_two, swap(normed_two, CORE)])
    sums, grads = None, []
    for up, dt, ub in (
        (up_own, dt_own, ub_own),
        (up_x, dt_x, ub_x),
        (up_y, dt_y, ub_y),
        (up_xy, dt_xy, ub_xy),
    ):
        *sums, dup, ddt, dub = run_feed_forward(pair, grad_pair, up, dt, ub.reshape(-1, 1), sums)
        grads.append((dup, ddt, jnp.sum(dub, axis=1)))
    out_sum, gn_sum = sums
    ffn_out = out_sum[0] + swap(out_sum[1].astype(bf16), CORE).astype(f32)
    grad_normed_two = gn_sum[0] + swap(gn_sum[1].astype(bf16), CORE).astype(f32)

    layer = (middle + (ffn_out + bias_down)).astype(bf16)
    layer_out = lax.all_to_all(layer.reshape(nn, part, quarter), "narrow", 0, 0, tiled=True)
    layer_out = layer_out.transpose(1, 0, 2).reshape(part, tok)

    (up_g, dt_g, ub_g), (up_gx, dt_gx, ub_gx), (up_gy, dt_gy, ub_gy), (up_gxy, dt_gxy, ub_gxy) = grads
    add = lambda *terms: sum(t.astype(f32) for t in terms)
    up_gy = add(up_gy, swap(up_gxy, X)).astype(bf16)
    dt_gx = add(dt_gx, swap(dt_gxy, Y)).astype(bf16)
    up_g = add(up_g, swap(up_gx, X), swap(up_gy, Y))
    dt_g = add(dt_g, swap(dt_gx, X), swap(dt_gy, Y))
    ub_g = ub_g + swap(ub_gx, X) + swap(ub_gy, Y) + swap(ub_gxy, X | Y)
    for bit in reversed(high):
        half = up_g.shape[1] // 2
        up_g = up_g[:, :half] + swap(up_g[:, half:].astype(bf16), bit).astype(f32)
        dt_g = dt_g[:, :half] + swap(dt_g[:, half:].astype(bf16), bit).astype(f32)
        ub_g = ub_g[:half] + swap(ub_g[half:], bit)
    up_grad = z_scatter_sum(up_g.astype(bf16).reshape(nn, part, -1))
    down_grad = z_scatter_sum(dt_g.astype(bf16).reshape(nn, part, -1)).T
    up_bias_grad = ub_g + sum(z_rotate(ub_g, r) for r in range(1, nn))

    grad_rows = grad_cols.astype(f32)
    grad_mid = grad_rows + norm_back(grad_normed_two, xhat_two, scale_two, gain_two)
    gain_two_grad = jnp.sum(grad_normed_two * xhat_two, axis=1)
    shift_two_grad = jnp.sum(grad_normed_two, axis=1)
    grad_branch = grad_mid.astype(bf16)
    out_bias_part = jnp.sum(grad_branch.astype(f32), axis=1)
    down_bias_part = jnp.sum(grad_rows, axis=1)
    grad_wo_t = mm(grad_branch, att, NT)
    grad_att = mm(wo_t, grad_branch, TN).astype(bf16)
    dqt, dk, dv = run_backward(
        starts, small, qt, q, kt, k, v, grad_att, grad_att.T, att, lse, segk, segq
    )
    grad_wq = mm(normed_own, dqt, NT)
    grad_wk = mm(normed, dk)
    grad_wv = mm(normed, dv)
    q_bias_part = jnp.sum(dqt.astype(f32), axis=1)
    v_bias_part = jnp.sum(dv.astype(f32), axis=0)
    grad_normed = mm(wk, dk, NT) + mm(wv, dv, NT) + jnp.pad(mm(wq, dqt), ((0, 0), (halo, halo)))
    gain_one_grad = jnp.sum(grad_normed * xhat_one, axis=1)
    shift_one_grad = jnp.sum(grad_normed, axis=1)
    grad_in = norm_back(grad_normed, xhat_one, scale_one, gain_one)
    grad_in = grad_in + jnp.pad(grad_mid, ((0, 0), (halo, halo)))
    grad_in = grad_in.astype(bf16).reshape(nn, part, span)
    grad_in = lax.all_to_all(grad_in, "narrow", 0, 0, tiled=True).astype(f32)
    tokens_grad = sum(
        jnp.pad(grad_in[j], ((0, 0), (j * quarter, tok - (j + 1) * quarter))) for j in range(nn)
    )[:, halo : halo + tok]

    attn_g = jnp.stack([grad_wq, grad_wk, grad_wv, grad_wo_t]).astype(bf16)
    attn_g = attn_g.reshape(4, nw, dw, D).transpose(1, 0, 2, 3)
    pick = lambda masks: jnp.concatenate(
        [lax.dynamic_index_in_dim(attn_g, mw ^ m, 0, True) for m in masks], axis=0
    )
    masks = [0]
    for bit in high:
        masks = masks + [m ^ bit for m in masks]
    count = len(masks)
    masks = [m ^ b for b in (0, X, Y, X | Y) for m in masks]
    half = add(pick(masks), swap(pick([m ^ CORE for m in masks]), CORE)).astype(bf16)
    g0, gx, gy, gxy = (half[i * count : (i + 1) * count] for i in range(4))
    gy_low = add(gy[:, :2], swap(gxy[:, :2], X)).astype(bf16)
    gx_high = add(gx[:, 2:], swap(gxy[:, 2:], Y)).astype(bf16)
    gx = jnp.concatenate([gx[:, :2], gx_high], axis=1)
    gy = jnp.concatenate([gy_low, gy[:, 2:]], axis=1)
    g0 = add(g0, swap(gx, X), swap(gy, Y))
    for bit in reversed(high):
        cut = g0.shape[0] // 2
        g0 = g0[:cut] + swap(g0[cut:].astype(bf16), bit).astype(f32)
    g0 = g0[0].astype(bf16).reshape(4, dw, nn, part).transpose(2, 0, 1, 3)
    attn_grad = z_scatter_sum(g0)
    qkv_grad = attn_grad[:3]
    out_weight_grad = attn_grad[3].T

    vector_rows = jnp.stack(
        [
            gain_one_grad,
            shift_one_grad,
            q_bias_part,
            v_bias_part,
            out_bias_part,
            gain_two_grad,
            shift_two_grad,
            down_bias_part,
        ]
    )
    vector_rows = z_scatter_sum(vector_rows.reshape(8, nn, part).transpose(1, 0, 2))
    class_ids = jnp.arange(CLASSES, dtype=jnp.int32)
    label_hits = labels[:, None] == class_ids
    counts = jnp.stack(
        [
            jnp.sum(((predicted[:, None] == class_ids) & label_hits).astype(f32), axis=0),
            jnp.sum(label_hits.astype(f32), axis=0),
        ]
    )
    counts = wide_sum(counts)
    vec = wide_sum(vector_rows)
    tallies = counts.astype(jnp.int32)
    accuracy = jnp.sum(counts[0]) / jnp.maximum(jnp.sum(counts[1]), 1.0)
    return (
        layer_out,
        tokens_grad,
        vec[0],
        vec[1],
        qkv_grad,
        vec[2:4],
        out_weight_grad,
        vec[4],
        vec[5],
        vec[6],
        up_grad,
        up_bias_grad,
        down_grad,
        vec[7],
        tallies,
        accuracy,
    )


def solution(mesh):
    return jax.shard_map(
        shards,
        mesh=mesh,
        in_specs=(
            P("narrow", "wide"),
            P("narrow"),
            P("narrow"),
            P(None, "wide", "narrow"),
            P(None, "narrow"),
            P("narrow", "wide"),
            P("narrow"),
            P("narrow"),
            P("narrow"),
            P("narrow", "wide"),
            P("wide"),
            P("wide", "narrow"),
            P("narrow"),
            P("wide"),
            P("narrow", "wide"),
            P("wide"),
            P("wide"),
        ),
        out_specs=(
            P("narrow", "wide"),
            P("narrow", "wide"),
            P("narrow"),
            P("narrow"),
            P(None, "wide", "narrow"),
            P(None, "narrow"),
            P("narrow", "wide"),
            P("narrow"),
            P("narrow"),
            P("narrow"),
            P("narrow", "wide"),
            P("wide"),
            P("wide", "narrow"),
            P("narrow"),
            P(),
            P(),
        ),
        check_vma=False,
    )
```

time: 1450 us -> 549 us (0.38)
  waiting for transfers between devices: 732 us -> 129 us
  matrix products: 438 us -> 24.4 us
  Pallas kernels: 0 us -> 140 us
  starting transfers between devices: 7.75 us -> 113 us
  blocking collectives: 89.9 us -> 0 us
  local copies, waits for them, and re-layouts: 95.1 us -> 51.9 us
    dot_general x31 -> x12, matrix products: 431 us -> 24.4 us  [mm(): return lax.dot_general(left, right, dims, preferred_element_type=f32)]
    all_gather x6 -> x0, waiting for transfers between devices: 257 us -> none  [the longest x1 110 us: shards(): lax.all_gather(up_piece, 'narrow', axis=0, tiled=True)]
    psum x1 -> x0, waiting for transfers between devices: 236 us -> none  [shards(): branch_sum = lax.psum(branch_part, 'narrow')]
    pallas_call x0 -> x6, Pallas kernels: none -> 140 us  [the longest x4 74.1 us: run_feed_forward(): pl.pallas_call(functools.partial(feed_forward, first), grid=(pair, rows /...]
    unnamed x20 -> x0, waiting for transfers between devices: 135 us -> none
    ppermute x0 -> x65, waiting for transfers between devices: none -> 98.4 us  [the longest x38 58.2 us: swap(): return lax.ppermute(x, 'wide', [(i, i ^ mask) for i in range(n)])]
    ppermute x0 -> x65, starting transfers between devices: none -> 92.7 us  [the longest x27 60.8 us: z_rotate(): return lax.ppermute(x, 'narrow', [(i, (i + k) % n) for i in range(n)])]
    reduce_scatter x3 -> x0, waiting for transfers between devices: 39.6 us -> none  [the longest x1 39.6 us: shards(): lax.psum_scatter(up_grad_mid, 'narrow', scatter_dimension=0, tiled=True)]
  transfers between devices with their start and end apart: 17 -> 69, of which waited for: 10 -> 19; matrix products, arithmetic and copies ran while one was open for 38% -> 23% of each run, Pallas kernels for 0% -> 22%
where the time goes in v1:
time: 549 us; the launch traced here: 543 us
  Pallas kernels  140 us (26%)
  waiting for transfers between devices  129 us (23%)
  starting transfers between devices  113 us (21%)
  other arithmetic  64.7 us (12%)
  local copies, waits for them, and re-layouts  51.9 us (9%)
  matrix products  24.4 us (4%)
  between operations  20.2 us (4%)
    pallas_call x4, Pallas kernels, run_feed_forward(): pl.pallas_call(functools.partial(feed_forward, first), grid=(pair, rows /...  74.1 us
    ppermute x27, starting transfers between devices, z_rotate(): return lax.ppermute(x, 'narrow', [(i, (i + k) % n) for i in range(n)])  60.8 us
    ppermute x38, waiting for transfers between devices, swap(): return lax.ppermute(x, 'wide', [(i, i ^ mask) for i in range(n)])  58.2 us
    ppermute x27, waiting for transfers between devices, z_rotate(): return lax.ppermute(x, 'narrow', [(i, (i + k) % n) for i in range(n)])  40.2 us
    pallas_call x1, Pallas kernels, run_backward(): pl.pallas_call(attend_backward, grid_spec=pltpu.PrefetchScalarGridSpec(nu...  34.3 us
    ppermute x38, starting transfers between devices, swap(): return lax.ppermute(x, 'wide', [(i, i ^ mask) for i in range(n)])  31.9 us
    pallas_call x1, Pallas kernels, run_forward(): pl.pallas_call(attend_forward, grid_spec=pltpu.PrefetchScalarGridSpec(num...  31.3 us
    all_to_all x1, waiting for transfers between devices, shards(): x_low = lax.all_to_all(blocks, 'narrow', 0, 0, tiled=True).reshape(D, span)  30.5 us
  transfers between devices with their start and end apart: 69, of which 19 were waited for; matrix products, arithmetic and copies ran while one was open for 23% of the time, Pallas kernels for 22%

profile of v1, /device:TPU:0, one launch (start us, length us, event | category | flops | bytes accessed | tf_op | source)
XLA Modules:
  0.0 542.9 jit_solution(16988177983646018477)
XLA Ops:
  3.1 5.0 collective-permute-start.2
  19.7 4.2 all-to-all-start.1
  25.4 3.8 collective-permute-start.10
  55.2 4.1 collective-permute-done.5
  67.8 8.8 %collective-permute-done.19 = bf16[160,640]{1,0:T(8,128)(2,1)S(1)} collective-permute-done((bf16[160,640]{1,0:T(8,128)(2,1)}, bf16[160,640]{1,0:T(8,128)(2,1)S(1)}, u32[]{:S(2)}, u32[]{:S(2)}) %collective-permute-start.19) | collective-permute-done | bytes 204832 | tf_op jit(solution)/shard_map/ppermute | solution.py:299
  76.6 4.7 collective-permute-start.15
  83.7 9.1 %all-to-all-start = ((bf16[4,160,1280]{2,1,0:T(8,128)(2,1)}), bf16[4,160,1280]{2,1,0:T(8,128)(2,1)S(1)}, u32[]{:S(2)}, u32[]{:S(2)}) async-start(bf16[4,160,1280]{2,1,0:T(8,128)(2,1)} %pad_maximum_fusion.3), calls=%async_computation | async-start | bytes 3276800 | tf_op jit(solution)/shard_map/all_to_all | solution.py:371
  102.3 30.5 %all-to-all-done = bf16[4,160,1280]{2,1,0:T(8,128)(2,1)S(1)} async-done(((bf16[4,160,1280]{2,1,0:T(8,128)(2,1)}), bf16[4,160,1280]{2,1,0:T(8,128)(2,1)S(1)}, u32[]{:S(2)}, u32[]{:S(2)}) %all-to-all-start) | async-done | bytes 1638432 | tf_op jit(solution)/shard_map/all_to_all | solution.py:371
  141.9 4.5 convolution_convert_fusion
  154.7 31.3 %attend_forward.1 = (bf16[640,768]{1,0:T(8,128)(2,1)}, f32[40,768]{1,0:T(8,128)}) custom-call(s32[3]{0:T(128)} %get-tuple-element.158.start_ref, s32[3]{0:T(128)} %get-tuple-element.159.small_ref, bf16[640,768]{1,0:T(8,128)(2,1)} %copy.88.q_ref.qt_ref, bf16[1280,640]{1,0:T(8,128)(2,1)} %bitcast.284, bf16[640,1280]{1,0:T(8,128)(2,1)} %copy.89.vt_ref, ...), custom_call_target="tpu_custom_call" | custom-call | flops 20000000000 | bytes 10000000 | tf_op jit(solution)/shard_map/attend_forward/pallas_call | solution.py:160
  224.0 18.1 %feed_forward.4 = (f32[2,640,768]{2,1,0:T(8,128)}, f32[2,640,768]{2,1,0:T(8,128)}, bf16[640,640]{1,0:T(8,128)(2,1)}, bf16[640,640]{1,0:T(8,128)(2,1)}, f32[640,128]{1,0:T(8,128)}) custom-call(bf16[2,640,768]{2,1,0:T(8,128)(2,1)} %pad_maximum_fusion.1.refs_0_, bf16[2,640,768]{2,1,0:T(8,128)(2,1)} %pad_maximum_fusion.2.refs_1_, ...), custom_call_target="tpu_custom_call" | custom-call | flops 7549747200 | bytes 20000000 | tf_op jit(solution)/shard_map/feed_forward/pallas_call | solution.py:255
  242.1 18.7 %feed_forward.5 = (f32[2,640,768]{2,1,0:T(8,128)}, f32[2,640,768]{2,1,0:T(8,128)}, bf16[640,640]{1,0:T(8,128)(2,1)}, bf16[640,640]{1,0:T(8,128)(2,1)}, f32[640,128]{1,0:T(8,128)}) custom-call(bf16[2,640,768]{2,1,0:T(8,128)(2,1)} %pad_maximum_fusion.1.refs_0_, ...), custom_call_target="tpu_custom_call", output_to_operand_aliasing={{0}: (5, {}), {1}: (6, {})} | custom-call | flops 7549747200 | bytes 20000000 | tf_op jit(solution)/shard_map/feed_forward/pallas_call | solution.py:255
  261.7 18.8 %feed_forward.6 = (f32[2,640,768]{2,1,0:T(8,128)}, f32[2,640,768]{2,1,0:T(8,128)}, bf16[640,640]{1,0:T(8,128)(2,1)}, bf16[640,640]{1,0:T(8,128)(2,1)}, f32[640,128]{1,0:T(8,128)}) custom-call(bf16[2,640,768]{2,1,0:T(8,128)(2,1)} %pad_maximum_fusion.1.refs_0_, ...), custom_call_target="tpu_custom_call", output_to_operand_aliasing={{0}: (5, {}), {1}: (6, {})} | custom-call | flops 7549747200 | bytes 20000000 | tf_op jit(solution)/shard_map/feed_forward/pallas_call | solution.py:255
  281.6 18.6 %feed_forward.7 = (f32[2,640,768]{2,1,0:T(8,128)}, f32[2,640,768]{2,1,0:T(8,128)}, bf16[640,640]{1,0:T(8,128)(2,1)}, bf16[640,640]{1,0:T(8,128)(2,1)}, f32[640,128]{1,0:T(8,128)}) custom-call(bf16[2,640,768]{2,1,0:T(8,128)(2,1)} %pad_maximum_fusion.1.refs_0_, ...), custom_call_target="tpu_custom_call", output_to_operand_aliasing={{0}: (5, {}), {1}: (6, {})} | custom-call | flops 7549747200 | bytes 20000000 | tf_op jit(solution)/shard_map/feed_forward/pallas_call | solution.py:255
  330.3 3.9 convert_reduce_fusion.3
  338.7 34.3 %attend_backward.1 = (bf16[640,768]{1,0:T(8,128)(2,1)}, bf16[1280,640]{1,0:T(8,128)(2,1)}, bf16[1280,640]{1,0:T(8,128)(2,1)}) custom-call(s32[3]{0:T(128)} %get-tuple-element.158.start_ref, s32[3]{0:T(128)} %get-tuple-element.159.small_ref, bf16[640,768]{1,0:T(8,128)(2,1)} %copy.88.q_ref.qt_ref, bf16[768,640]{1,0:T(8,128)(2,1)} %bitcast.288, ...), custom_call_target="tpu_custom_call" | custom-call | flops 40000000000 | bytes 20000000 | tf_op jit(solution)/shard_map/attend_backward/pallas_call | solution.py:182
  408.2 30.7 %collective-permute-done.34 = f32[8,160]{1,0:T(8,128)S(1)} collective-permute-done((f32[8,160]{1,0:T(8,128)S(1)}, f32[8,160]{1,0:T(8,128)S(1)}, u32[]{:S(2)}, u32[]{:S(2)}) %collective-permute-start.34) | collective-permute-done | bytes 5152 | tf_op jit(solution)/shard_map/ppermute | solution.py:319
  438.9 4.8 add_convert_fusion.2
  458.8 8.2 %collective-permute-done.37 = bf16[1,2,80,640]{3,2,1,0:T(8,128)(2,1)S(1)} collective-permute-done((bf16[1,2,80,640]{3,2,1,0:T(8,128)(2,1)}, bf16[1,2,80,640]{3,2,1,0:T(8,128)(2,1)S(1)}, u32[]{:S(2)}, u32[]{:S(2)}) %collective-permute-start.37) | collective-permute-done | bytes 204832 | tf_op jit(solution)/shard_map/ppermute | solution.py:319
  475.0 15.6 %collective-permute-done.59 = bf16[160,640]{1,0:T(8,128)(2,1)S(1)} collective-permute-done((bf16[160,640]{1,0:T(8,128)(2,1)S(1)}, bf16[160,640]{1,0:T(8,128)(2,1)S(1)}, u32[]{:S(2)}, u32[]{:S(2)}) %collective-permute-start.59) | collective-permute-done | bytes 204832 | tf_op jit(solution)/shard_map/ppermute | solution.py:299
  490.6 15.2 %collective-permute-start.47 = (bf16[160,640]{1,0:T(8,128)(2,1)}, bf16[160,640]{1,0:T(8,128)(2,1)}, u32[]{:S(2)}, u32[]{:S(2)}) collective-permute-start(bf16[160,640]{1,0:T(8,128)(2,1)} %get-tuple-element.196), channel_id=1, source_target_pairs={{0,1},{1,2},{2,3},{3,0},{4,5},{5,6},{6,7},{7,4},{8,9},{9,10},{10,1... | collective-permute-start | bytes 614408 | tf_op jit(solution)/shard_map/ppermute | solution.py:299
  505.9 6.0 %collective-permute-done.60 = bf16[160,640]{1,0:T(8,128)(2,1)S(1)} collective-permute-done((bf16[160,640]{1,0:T(8,128)(2,1)S(1)}, bf16[160,640]{1,0:T(8,128)(2,1)S(1)}, u32[]{:S(2)}, u32[]{:S(2)}) %collective-permute-start.60) | collective-permute-done | bytes 204832 | tf_op jit(solution)/shard_map/ppermute | solution.py:299
  518.5 4.6 collective-permute-start.41
  532.1 5.7 %collective-permute-done.42 = bf16[4,80,160]{2,1,0:T(8,128)(2,1)S(1)} collective-permute-done((bf16[4,80,160]{2,1,0:T(8,128)(2,1)S(1)}, bf16[4,80,160]{2,1,0:T(8,128)(2,1)S(1)}, u32[]{:S(2)}, u32[]{:S(2)}) %collective-permute-start.42) | collective-permute-done | bytes 102432 | tf_op jit(solution)/shard_map/ppermute | solution.py:299
  (377 shorter events, 213.4 us)
Async XLA Ops:
  13.8 48.1 %collective-permute-start.8 = (bf16[8,160]{1,0:T(8,128)(2,1)S(1)}, bf16[8,160]{1,0:T(8,128)(2,1)S(1)}, u32[]{:S(2)}, u32[]{:S(2)}) collective-permute-start(bf16[8,160]{1,0:T(8,128)(2,1)S(1)} %stack.190), channel_id=1, source_target_pairs={{0,1},{1,2},{2,3},{3,0},{4,5},{5,6},{6,7},{7,4},{8,9},{9,10},{10,1... | collective-permute-start | bytes 7688 | tf_op jit(solution)/shard_map/ppermute | solution.py:299
  17.3 45.2 %collective-permute-start.9 = (bf16[8,160]{1,0:T(8,128)(2,1)S(1)}, bf16[8,160]{1,0:T(8,128)(2,1)S(1)}, u32[]{:S(2)}, u32[]{:S(2)}) collective-permute-start(bf16[8,160]{1,0:T(8,128)(2,1)S(1)} %stack.190), channel_id=1, source_target_pairs={{0,2},{1,3},{2,0},{3,1},{4,6},{5,7},{6,4},{7,5},{8,10},{9,11},{10,... | collective-permute-start | bytes 7688 | tf_op jit(solution)/shard_map/ppermute | solution.py:299
  19.7 63.9 %all-to-all-start.1 = ((bf16[4,160,768]{2,1,0:T(8,128)(2,1)}), bf16[4,160,768]{2,1,0:T(8,128)(2,1)S(1)}, u32[]{:S(2)}, u32[]{:S(2)}) async-start(bf16[4,160,768]{2,1,0:T(8,128)(2,1)} %pad_maximum_fusion.5), calls=%async_computation.1 | async-start | bytes 1966080 | tf_op jit(solution)/shard_map/all_to_all | solution.py:411
  25.4 39.8 %collective-permute-start.10 = (bf16[8,160]{1,0:T(8,128)(2,1)S(1)}, bf16[8,160]{1,0:T(8,128)(2,1)S(1)}, u32[]{:S(2)}, u32[]{:S(2)}) collective-permute-start(bf16[8,160]{1,0:T(8,128)(2,1)S(1)} %stack.190), channel_id=1, source_target_pairs={{0,3},{1,0},{2,1},{3,2},{4,7},{5,4},{6,5},{7,6},{8,11},{9,8},{10,9... | collective-permute-start | bytes 7688 | tf_op jit(solution)/shard_map/ppermute | solution.py:299
  61.3 37.3 %collective-permute-start.7 = (bf16[4,4,80,640]{3,2,1,0:T(8,128)(2,1)}, bf16[4,4,80,640]{3,2,1,0:T(8,128)(2,1)}, u32[]{:S(2)}, u32[]{:S(2)}) collective-permute-start(bf16[4,4,80,640]{3,2,1,0:T(8,128)(2,1)} %maximum_maximum_fusion), channel_id=1, source_target_pairs={{0,4},{4,0},{8,12},{12,8},{16,20},{20,16},{24,28},{28,24},{1,5},{5... | collective-permute-start | bytes 4915208 | tf_op jit(solution)/shard_map/ppermute | solution.py:319
  81.6 111.1 %collective-permute-start.63 = (f32[2,4]{1,0:T(2,128)S(1)}, f32[2,4]{1,0:T(2,128)S(1)}, u32[]{:S(2)}, u32[]{:S(2)}) collective-permute-start(f32[2,4]{1,0:T(2,128)S(1)} %fusion.56), channel_id=1, source_target_pairs={{0,8},{4,12},{8,0},{12,4},{16,24},{20,28},{24,16},{28,20},{1,9},{5... | collective-permute-start | bytes 104 | tf_op jit(solution)/shard_map/ppermute | solution.py:319
  83.7 49.2 %all-to-all-start = ((bf16[4,160,1280]{2,1,0:T(8,128)(2,1)}), bf16[4,160,1280]{2,1,0:T(8,128)(2,1)S(1)}, u32[]{:S(2)}, u32[]{:S(2)}) async-start(bf16[4,160,1280]{2,1,0:T(8,128)(2,1)} %pad_maximum_fusion.3), calls=%async_computation | async-start | bytes 3276800 | tf_op jit(solution)/shard_map/all_to_all | solution.py:371
  96.1 119.3 %collective-permute-start.21 = (bf16[640,640]{1,0:T(8,128)(2,1)}, bf16[640,640]{1,0:T(8,128)(2,1)}, u32[]{:S(2)}, u32[]{:S(2)}) collective-permute-start(bf16[640,640]{1,0:T(8,128)(2,1)} %pad_maximum_fusion.9.refs_3_), channel_id=1, source_target_pairs={{0,8},{4,12},{8,0},{12,4},{16,24},{20,28},{24,16},{28,20},{1,9},{5... | collective-permute-start | bytes 2457608 | tf_op jit(solution)/shard_map/ppermute | solution.py:319
  97.8 119.7 %collective-permute-start.16 = (bf16[640,640]{1,0:T(8,128)(2,1)}, bf16[640,640]{1,0:T(8,128)(2,1)}, u32[]{:S(2)}, u32[]{:S(2)}) collective-permute-start(bf16[640,640]{1,0:T(8,128)(2,1)} %pad_maximum_fusion.7.refs_2_), channel_id=1, source_target_pairs={{0,16},{4,20},{8,24},{12,28},{16,0},{20,4},{24,8},{28,12},{1,17},{... | collective-permute-start | bytes 2457608 | tf_op jit(solution)/shard_map/ppermute | solution.py:319
  98.5 119.0 %collective-permute-start.12 = (bf16[640,768]{1,0:T(8,128)(2,1)S(1)}, bf16[640,768]{1,0:T(8,128)(2,1)}, u32[]{:S(2)}, u32[]{:S(2)}) collective-permute-start(bf16[640,768]{1,0:T(8,128)(2,1)S(1)} %bitcast.266), channel_id=1, source_target_pairs={{0,4},{4,0},{8,12},{12,8},{16,20},{20,16},{24,28},{28,24},{1,5},{5... | collective-permute-start | bytes 2949128 | tf_op jit(solution)/shard_map/ppermute | solution.py:319
  215.4 45.4 %collective-permute-start.24 = (bf16[640,640]{1,0:T(8,128)(2,1)}, bf16[640,640]{1,0:T(8,128)(2,1)S(1)}, u32[]{:S(2)}, u32[]{:S(2)}) collective-permute-start(bf16[640,640]{1,0:T(8,128)(2,1)} %pad_maximum_fusion.9.refs_3_), channel_id=1, source_target_pairs={{0,16},{4,20},{8,24},{12,28},{16,0},{20,4},{24,8},{28,12},{1,17},{... | collective-permute-start | bytes 2457608 | tf_op jit(solution)/shard_map/ppermute | solution.py:319
  217.5 63.0 %collective-permute-start.17 = (bf16[640,640]{1,0:T(8,128)(2,1)}, bf16[640,640]{1,0:T(8,128)(2,1)S(1)}, u32[]{:S(2)}, u32[]{:S(2)}) collective-permute-start(bf16[640,640]{1,0:T(8,128)(2,1)} %collective-permute-done.16.refs_2_), channel_id=1, source_target_pairs={{0,8},{4,12},{8,0},{12,4},{16,24},{20,28},{24,16},{28,20},{1,9},{5... | collective-permute-start | bytes 2457608 | tf_op jit(solution)/shard_map/ppermute | solution.py:319
  217.5 63.0 %collective-permute-start.22 = (bf16[640,640]{1,0:T(8,128)(2,1)}, bf16[640,640]{1,0:T(8,128)(2,1)S(1)}, u32[]{:S(2)}, u32[]{:S(2)}) collective-permute-start(bf16[640,640]{1,0:T(8,128)(2,1)} %collective-permute-done.21.refs_3_), channel_id=1, source_target_pairs={{0,16},{4,20},{8,24},{12,28},{16,0},{20,4},{24,8},{28,12},{1,17},{... | collective-permute-start | bytes 2457608 | tf_op jit(solution)/shard_map/ppermute | solution.py:319
  321.4 132.8 %collective-permute-start.58 = (bf16[640,640]{1,0:T(8,128)(2,1)}, bf16[640,640]{1,0:T(8,128)(2,1)}, u32[]{:S(2)}, u32[]{:S(2)}) collective-permute-start(bf16[640,640]{1,0:T(8,128)(2,1)} %get-tuple-element.65), channel_id=1, source_target_pairs={{0,16},{4,20},{8,24},{12,28},{16,0},{20,4},{24,8},{28,12},{1,17},{... | collective-permute-start | bytes 2457608 | tf_op jit(solution)/shard_map/ppermute | solution.py:319
  323.0 72.3 %collective-permute-start.45 = (bf16[640,640]{1,0:T(8,128)(2,1)}, bf16[640,640]{1,0:T(8,128)(2,1)}, u32[]{:S(2)}, u32[]{:S(2)}) collective-permute-start(bf16[640,640]{1,0:T(8,128)(2,1)} %get-tuple-element.57), channel_id=1, source_target_pairs={{0,8},{4,12},{8,0},{12,4},{16,24},{20,28},{24,16},{28,20},{1,9},{5... | collective-permute-start | bytes 2457608 | tf_op jit(solution)/shard_map/ppermute | solution.py:319
  385.8 61.0 %collective-permute-start.36 = (bf16[4,4,80,640]{3,2,1,0:T(8,128)(2,1)}, bf16[4,4,80,640]{3,2,1,0:T(8,128)(2,1)}, u32[]{:S(2)}, u32[]{:S(2)}) collective-permute-start(bf16[4,4,80,640]{3,2,1,0:T(8,128)(2,1)} %pad_maximum_fusion.4), channel_id=1, source_target_pairs={{0,4},{4,0},{8,12},{12,8},{16,20},{20,16},{24,28},{28,24},{1,5},{5... | collective-permute-start | bytes 4915208 | tf_op jit(solution)/shard_map/ppermute | solution.py:319
  401.3 68.9 %collective-permute-start.44 = (bf16[640,640]{1,0:T(8,128)(2,1)}, bf16[640,640]{1,0:T(8,128)(2,1)}, u32[]{:S(2)}, u32[]{:S(2)}) collective-permute-start(bf16[640,640]{1,0:T(8,128)(2,1)} %get-tuple-element.55), channel_id=1, source_target_pairs={{0,8},{4,12},{8,0},{12,4},{16,24},{20,28},{24,16},{28,20},{1,9},{5... | collective-permute-start | bytes 2457608 | tf_op jit(solution)/shard_map/ppermute | solution.py:319
  401.3 53.3 %collective-permute-start.57 = (bf16[640,640]{1,0:T(8,128)(2,1)}, bf16[640,640]{1,0:T(8,128)(2,1)}, u32[]{:S(2)}, u32[]{:S(2)}) collective-permute-start(bf16[640,640]{1,0:T(8,128)(2,1)} %add_convert_fusion.7), channel_id=1, source_target_pairs={{0,8},{4,12},{8,0},{12,4},{16,24},{20,28},{24,16},{28,20},{1,9},{5... | collective-permute-start | bytes 2457608 | tf_op jit(solution)/shard_map/ppermute | solution.py:319
  404.7 46.0 %all-to-all-start.2 = ((bf16[4,160,768]{2,1,0:T(8,128)(2,1)}), bf16[4,160,768]{2,1,0:T(8,128)(2,1)S(1)}, u32[]{:S(2)}, u32[]{:S(2)}) async-start(bf16[4,160,768]{2,1,0:T(8,128)(2,1)} %bitcast.70), calls=%async_computation.2 | async-start | bytes 1966080 | tf_op jit(solution)/shard_map/all_to_all | solution.py:459
  450.7 88.6 %all-to-all-start.3 = ((bf16[4,160,1280]{2,1,0:T(8,128)(2,1)}), bf16[4,160,1280]{2,1,0:T(8,128)(2,1)S(1)}, u32[]{:S(2)}, u32[]{:S(2)}) async-start(bf16[4,160,1280]{2,1,0:T(8,128)(2,1)} %bitcast.273), calls=%async_computation.3 | async-start | bytes 3276800 | tf_op jit(solution)/shard_map/all_to_all | solution.py:501
  467.0 44.8 %collective-permute-start.60 = (bf16[160,640]{1,0:T(8,128)(2,1)S(1)}, bf16[160,640]{1,0:T(8,128)(2,1)S(1)}, u32[]{:S(2)}, u32[]{:S(2)}) collective-permute-start(bf16[160,640]{1,0:T(8,128)(2,1)S(1)} %get-tuple-element.195), channel_id=1, source_target_pairs={{0,2},{1,3},{2,0},{3,1},{4,6},{5,7},{6,4},{7,5},{8,10},{9,11},{10,... | collective-permute-start | bytes 614408 | tf_op jit(solution)/shard_map/ppermute | solution.py:299
  468.5 43.4 %collective-permute-start.61 = (bf16[160,640]{1,0:T(8,128)(2,1)S(1)}, bf16[160,640]{1,0:T(8,128)(2,1)S(1)}, u32[]{:S(2)}, u32[]{:S(2)}) collective-permute-start(bf16[160,640]{1,0:T(8,128)(2,1)S(1)} %get-tuple-element.194), channel_id=1, source_target_pairs={{0,3},{1,0},{2,1},{3,2},{4,7},{5,4},{6,5},{7,6},{8,11},{9,8},{10,9... | collective-permute-start | bytes 614408 | tf_op jit(solution)/shard_map/ppermute | solution.py:299
  470.2 44.3 %collective-permute-start.38 = (bf16[1,4,80,640]{3,2,1,0:T(8,128)(2,1)S(1)}, bf16[1,4,80,640]{3,2,1,0:T(8,128)(2,1)S(1)}, u32[]{:S(2)}, u32[]{:S(2)}) collective-permute-start(bf16[1,4,80,640]{3,2,1,0:T(8,128)(2,1)S(1)} %pad_maximum_fusion.11), channel_id=1, source_target_pairs={{0,8},{4,12},{8,0},{12,4},{16,24},{20,28},{24,16},{28,20},{1,9},{5... | collective-permute-start | bytes 1228808 | tf_op jit(solution)/shard_map/ppermute | solution.py:319
  471.2 43.3 %collective-permute-start.40 = (bf16[1,4,80,640]{3,2,1,0:T(8,128)(2,1)S(1)}, bf16[1,4,80,640]{3,2,1,0:T(8,128)(2,1)S(1)}, u32[]{:S(2)}, u32[]{:S(2)}) collective-permute-start(bf16[1,4,80,640]{3,2,1,0:T(8,128)(2,1)S(1)} %pad_maximum_fusion.12), channel_id=1, source_target_pairs={{0,16},{4,20},{8,24},{12,28},{16,0},{20,4},{24,8},{28,12},{1,17},{... | collective-permute-start | bytes 1228808 | tf_op jit(solution)/shard_map/ppermute | solution.py:319
  (92 other events, 922.6 us)
